TPU v7x, 128 devices: a whole 4x4x4 slice. The times are simulated.
128 devices in a mesh: lat: 4 (over y_hi, core), lon: 32 (over x, y_lo, z).
Axes of the slice: x: 4, y: 4 (y_hi: 2, y_lo: 2; y = y_hi * 2 + y_lo), z: 4, core: 2. Of those that a mesh axis runs over, the one named last changes fastest.
Arguments:
- query_states: bfloat16 [16384, 512], P(('lat', 'lon')), may hold values from -41 to 41
- key_states: bfloat16 [16384, 512], P(('lat', 'lon')), may hold values from -17 to 17
- silu_slope: bfloat16 [16384, 2048], P(('lat', 'lon')), may hold values from -0.099609375 to 1.09375
- w_value: bfloat16 [512, 512], replicated, may hold values from -0.25 to 0.25
- w_out: bfloat16 [512, 512], replicated, may hold values from -0.5 to 0.5
- w_up: bfloat16 [512, 2048], replicated, may hold values from -0.25 to 0.25
- w_down: bfloat16 [2048, 512], replicated, may hold values from -0.125 to 0.125
- w_obs: bfloat16 [512, 128], replicated, may hold values from -0.25 to 0.25
- obs_cells: int32 [4, 32, 4, 4, 128], P('lat', 'lon'), may hold values from 0 to 127
- obs_weights: float32 [4, 32, 4, 4, 128], P('lat', 'lon'), may hold values from 0.05 to 0.5
- obs_count: int32 [4, 32, 4], P('lat', 'lon'), may hold values from 32 to 128, as said below
- innovations: float32 [4, 32, 128, 4, 128], P('lat', 'lon'), may hold values from -13 to 13
- obs_precision: float32 [128], replicated, may hold values from 0.3 to 3
Outputs:
- solution: float32 [16384, 512], P(('lat', 'lon'))
- residual: float32 [16384, 512], P(('lat', 'lon'))
Inputs may be any that keep to these rules, and one draw needn't show every extreme that they name: `obs_count`: in every draw, for each longitude sector, one latitude band receives 128 live slots from every device of that sector.
All inputs are finite; a program needn't handle non-finite values.
Results may differ from a plain program's by a relative error of at most 0.034.
Values may be sent and summed in bfloat16 or wider, within the bound.
A program may use at most 128 MiB of HBM per device.

v0:
```python
import math

import jax
import jax.numpy as jnp
from jax import lax
from jax.sharding import PartitionSpec as P

D = 512
HEADS = 8
HEAD_DIM = 64
STENCIL = 4
ITERS = 2
SLOTS = 128


def for_sending(x):
    return jax.tree.map(lambda a: a.astype(jnp.bfloat16) if a.dtype == jnp.float32 else a, x)


def head_scores(query_part, key_part):
    head_scale = 1.0 / math.sqrt(HEAD_DIM)
    return (
        jnp.einsum("thd,shd->hts", query_part, key_part, preferred_element_type=jnp.float32)
        * head_scale
    )


def with_heads(matrix):
    return matrix.reshape(matrix.shape[0], HEADS, HEAD_DIM)


def operator_matrix(stencil_rows, row_count):
    cell_index = stencil_rows[:STENCIL].reshape(-1).astype(jnp.int32)
    weight = stencil_rows[STENCIL:].reshape(-1)
    matches = (
        lax.broadcasted_iota(jnp.int32, (row_count, cell_index.shape[0]), 0) == cell_index[None, :]
    )
    return matches.astype(jnp.float32) * weight[None, :]


def forward_values(matrix, field_rows):
    product = lax.dot_general(
        field_rows,
        matrix,
        (((0,), (0,)), ((), ())),
        precision=lax.Precision.HIGHEST,
        preferred_element_type=jnp.float32,
    )
    return product.reshape(product.shape[0], STENCIL, -1, SLOTS).sum(axis=1)


def adjoint_values(matrix, errors):
    widened = jnp.broadcast_to(
        errors[:, None], (errors.shape[0], STENCIL) + errors.shape[1:]
    ).reshape(errors.shape[0], -1)
    return lax.dot_general(
        matrix,
        widened,
        (((1,), (1,)), ((), ())),
        precision=lax.Precision.HIGHEST,
        preferred_element_type=jnp.float32,
    )


def per_device(
    query_states,
    key_states,
    silu_slope,
    w_value,
    w_out,
    w_up,
    w_down,
    w_obs,
    obs_cells,
    obs_weights,
    obs_count,
    innovations,
    obs_precision,
):
    tok_rows = query_states.shape[0]
    lat_count = lax.axis_size("lat")
    local_query = with_heads(query_states)
    local_key = with_heads(key_states)

    def fold_total(accumulated, shard_rows):
        top_score, running = accumulated
        scores = head_scores(local_query, with_heads(shard_rows))
        raised = jnp.maximum(top_score, jnp.max(scores, axis=2))
        running = running * jnp.exp(top_score - raised) + jnp.sum(
            jnp.exp(scores - raised[:, :, None]), axis=2
        )
        return (raised, running)

    start_top = jnp.full((HEADS, tok_rows), -jnp.inf, jnp.float32)
    start_sum = jnp.zeros((HEADS, tok_rows), jnp.float32)
    band_query, band_key = (
        lax.all_gather(query_states, "lon", axis=0, tiled=True),
        lax.all_gather(key_states, "lon", axis=0, tiled=True),
    )
    band_rows = band_key.shape[0]
    block_rows = math.gcd(band_rows, 512)
    key_blocks = band_key.reshape(band_rows // block_rows, block_rows, D)

    def scan_total(accumulated, block):
        return (fold_total(accumulated, block), None)

    (top_score, running), unused = lax.scan(scan_total, (start_top, start_sum), key_blocks)
    log_local = top_score + jnp.log(running)
    band_log = lax.all_gather(log_local, "lon", axis=1, tiled=True)

    def mix_back(query_part, log_part, upward_part):
        scores = head_scores(local_key, query_part)
        frozen = jnp.exp(scores - log_part[:, None, :]).astype(jnp.bfloat16)
        return jnp.einsum(
            "hts,shd->thd", frozen, with_heads(upward_part), preferred_element_type=jnp.float32
        )

    def spread_back(upward):
        summed = mix_back(
            with_heads(band_query), band_log, lax.all_gather(upward, "lon", axis=0, tiled=True)
        )
        return summed.reshape(tok_rows, D).astype(jnp.bfloat16)

    def adjoint_model(gradient):
        back_hidden = (
            jnp.dot(gradient.astype(jnp.bfloat16), w_down.T, preferred_element_type=jnp.float32)
            * silu_slope
        ).astype(jnp.bfloat16)
        middle = gradient + jnp.dot(back_hidden, w_up.T, preferred_element_type=jnp.float32)
        upward = jnp.dot(
            middle.astype(jnp.bfloat16), w_out.T, preferred_element_type=jnp.float32
        ).astype(jnp.bfloat16)
        return middle + jnp.dot(spread_back(upward), w_value.T, preferred_element_type=jnp.float32)

    cell_ids = obs_cells[0, 0]
    live_slots = (
        lax.broadcasted_iota(jnp.int32, (lat_count, SLOTS), 1) < obs_count[0, 0][:, None]
    ).astype(jnp.float32)
    masked = obs_weights[0, 0] * live_slots[None]
    stencil = jnp.concatenate([cell_ids.astype(jnp.float32), masked], axis=0)

    def observe_adjoint(errors):
        arrived = lax.all_to_all(
            for_sending(jnp.concatenate([stencil, errors], axis=0)),
            "lat",
            split_axis=1,
            concat_axis=1,
            tiled=True,
        )
        grad_field = adjoint_values(
            operator_matrix(arrived[: 2 * STENCIL], tok_rows), arrived[2 * STENCIL :]
        )
        return jnp.dot(grad_field.astype(jnp.bfloat16), w_obs.T, preferred_element_type=jnp.float32)

    def squares(vector):
        return lax.psum(jnp.sum(vector * vector), ("lat", "lon"))

    precision = obs_precision[:, None, None]
    right_side = adjoint_model(observe_adjoint(precision * innovations[0, 0]))
    solution = jnp.zeros_like(right_side)
    residual = right_side
    direction = right_side
    norm_now = squares(residual)
    for iteration in range(ITERS):
        tangent_values = jnp.dot(
            direction.astype(jnp.bfloat16), w_value, preferred_element_type=jnp.float32
        ).astype(jnp.bfloat16)
        mix_scores = head_scores(local_query, with_heads(band_key))
        mix_frozen = jnp.exp(mix_scores - log_local[:, :, None]).astype(jnp.bfloat16)
        attend_summed = jnp.einsum(
            "hts,shd->thd",
            mix_frozen,
            with_heads(lax.all_gather(tangent_values, "lon", axis=0, tiled=True)),
            preferred_element_type=jnp.float32,
        )
        after_attention = direction + jnp.dot(
            attend_summed.reshape(tok_rows, D).astype(jnp.bfloat16),
            w_out,
            preferred_element_type=jnp.float32,
        )
        hidden = (
            jnp.dot(after_attention.astype(jnp.bfloat16), w_up, preferred_element_type=jnp.float32)
            * silu_slope
        ).astype(jnp.bfloat16)
        field_cols = jnp.dot(
            (after_attention + jnp.dot(hidden, w_down, preferred_element_type=jnp.float32)).astype(
                jnp.bfloat16
            ),
            w_obs,
            preferred_element_type=jnp.float32,
        )
        observe_arrived = lax.all_to_all(stencil, "lat", split_axis=1, concat_axis=1, tiled=True)
        applied = direction + adjoint_model(
            observe_adjoint(
                precision
                * lax.all_to_all(
                    forward_values(operator_matrix(observe_arrived, tok_rows), field_cols).astype(
                        jnp.bfloat16
                    ),
                    "lat",
                    split_axis=1,
                    concat_axis=1,
                    tiled=True,
                ).astype(jnp.float32)
            )
        )
        step_size = norm_now / lax.psum(jnp.sum(direction * applied), ("lat", "lon"))
        solution = solution + step_size * direction
        residual = residual - step_size * applied
        norm_next = squares(residual)
        direction = residual + norm_next / norm_now * direction
        norm_now = norm_next
    return (solution, residual)


def solution(mesh):
    in_specs = (
        P(("lat", "lon"), None),
        P(("lat", "lon"), None),
        P(("lat", "lon"), None),
        P(),
        P(),
        P(),
        P(),
        P(),
        P("lat", "lon", None, None, None),
        P("lat", "lon", None, None, None),
        P("lat", "lon", None),
        P("lat", "lon", None, None, None),
        P(),
    )
    out_specs = (P(("lat", "lon"), None), P(("lat", "lon"), None))
    return jax.shard_map(
        per_device, mesh=mesh, in_specs=in_specs, out_specs=out_specs, check_vma=False
    )
```

profile of v0, /device:TPU:0, one launch (start us, length us, event | category | flops | bytes accessed | tf_op | source)
XLA Modules:
  0.0 1484.7 jit_solution(4080322928281371864)
XLA Ops:
  13.1 4.5 all-to-all-start
  35.4 134.3 %all-gather.10.cloned.1.call-done = bf16[4096,512]{1,0:T(8,128)(2,1)} async-done(((bf16[128,512]{1,0:T(8,128)(2,1)}), bf16[4096,512]{1,0:T(8,128)(2,1)}) %all-gather.10.cloned.1.call-update) | async-done | bytes 4194320 | tf_op jit(solution)/shard_map/all_gather | solution.py:97
  169.7 6.4 copy.82
  176.1 152.1 %all-gather.12.cloned.1.call-done = bf16[4096,512]{1,0:T(8,128)(2,1)} async-done(((bf16[128,512]{1,0:T(8,128)(2,1)}), bf16[4096,512]{1,0:T(8,128)(2,1)}) %all-gather.12.cloned.1.call-update) | async-done | bytes 4194320 | tf_op jit(solution)/shard_map/all_gather | solution.py:98
  328.3 17.9 %while.13 = (s32[]{:T(128)}, f32[8,128]{1,0:T(8,128)S(1)}, f32[8,128]{1,0:T(8,128)S(1)}, bf16[8,512,512]{2,1,0:T(8,128)(2,1)}, bf16[128,8,64]{0,2,1:T(8,128)(2,1)S(1)}, /*index=5*/s32[]{:T(128)}, s32[]{:T(128)}) while((s32[]{:T(128)}, f32[8,128]{1,0:T(8,128)S(1)}, f32[8,128]{1,0:T(8,128)S(1)}, bf16[8,512,512]{2,1,0:T(8,128)(2,1)}, ...), condition=%wide.region_3.4_spmd.clone, body=%wide.region_0.3_spmd.clone.sunk | while | flops 69735424 | bytes 7000164 | solution.py:107
  346.2 81.0 %all_gather.27 = f32[8,4096]{1,0:T(8,128)S(1)} all-gather(f32[8,128]{1,0:T(8,128)S(1)} %log_add_fusion), channel_id=1, replica_groups=mesh['lat'=4,'lon'=32] {'lon'}, dimensions={1}, use_global_device_ids=true | all-gather | bytes 135168 | tf_op jit(solution)/shard_map/all_gather | solution.py:109
  427.2 8.4 exponential_convert_fusion.1
  435.6 51.8 %all-gather.8.cloned.1.call-done = bf16[4096,512]{1,0:T(8,128)(2,1)} async-done(((bf16[128,512]{1,0:T(8,128)(2,1)}), bf16[4096,512]{1,0:T(8,128)(2,1)}) %all-gather.8.cloned.1.call-update) | async-done | bytes 4194320 | tf_op jit(solution)/shard_map/all_gather | solution.py:120
  487.4 6.4 copy.80
  493.8 7.7 convolution_convert_fusion.8
  502.9 9.7 all_to_all.31
  512.6 6.4 copy.86
  519.1 8.4 exponential_convert_fusion
  527.5 132.9 %all-gather.14.cloned.1.call-done = bf16[4096,512]{1,0:T(8,128)(2,1)} async-done(((bf16[128,512]{1,0:T(8,128)(2,1)}), bf16[4096,512]{1,0:T(8,128)(2,1)}) %all-gather.14.cloned.1.call-update) | async-done | bytes 4194320 | tf_op jit(solution)/shard_map/all_gather | solution.py:173
  660.4 6.4 copy.85
  666.8 7.7 convolution_convert_fusion.6
  687.7 9.9 all_to_all.32
  699.1 8.6 all_to_all.33
  721.0 155.2 %all-gather.16.cloned.1.call-done = bf16[4096,512]{1,0:T(8,128)(2,1)} async-done(((bf16[128,512]{1,0:T(8,128)(2,1)}), bf16[4096,512]{1,0:T(8,128)(2,1)}) %all-gather.16.cloned.1.call-update) | async-done | bytes 4194320 | tf_op jit(solution)/shard_map/all_gather | solution.py:120
  876.1 6.4 copy.93
  882.5 7.7 convolution_convert_fusion.4
  891.9 63.5 %all-reduce = (f32[]{:T(128)}, f32[]{:T(128)}) all-reduce(f32[]{:T(128)} %get-tuple-element.71, f32[]{:T(128)} %get-tuple-element.70), channel_id=1, replica_groups=mesh['lat'=4,'lon'=32] {'lat','lon'}, use_global_device_ids=true, to_apply=%region_5.6 | all-reduce | flops 2 | bytes 16 | tf_op jit(solution)/shard_map/psum | solution.py:156
  958.3 65.0 %psum.30 = f32[]{:T(128)} all-reduce(f32[]{:T(128)} %multiply_reduce_fusion.1), channel_id=1, replica_groups=mesh['lat'=4,'lon'=32] {'lat','lon'}, use_global_device_ids=true, to_apply=%region_10.11 | all-reduce | flops 1 | bytes 8 | tf_op jit(solution)/shard_map/psum | solution.py:156
  1028.3 153.6 %all-gather.18.cloned.1.call-done = bf16[4096,512]{1,0:T(8,128)(2,1)} async-done(((bf16[128,512]{1,0:T(8,128)(2,1)}), bf16[4096,512]{1,0:T(8,128)(2,1)}) %all-gather.18.cloned.1.call-update) | async-done | bytes 4194320 | tf_op jit(solution)/shard_map/all_gather | solution.py:173
  1182.0 6.4 copy.94
  1188.4 7.7 convolution_convert_fusion.2
  1209.3 9.9 all_to_all.34
  1220.7 8.8 all_to_all.35
  1241.4 155.4 %all-gather.20.cloned.1.call-done = bf16[4096,512]{1,0:T(8,128)(2,1)} async-done(((bf16[128,512]{1,0:T(8,128)(2,1)}), bf16[4096,512]{1,0:T(8,128)(2,1)}) %all-gather.20.cloned.1.call-update) | async-done | bytes 4194320 | tf_op jit(solution)/shard_map/all_gather | solution.py:120
  1396.8 6.4 copy.99
  1403.2 7.7 convolution_convert_fusion
  1411.9 63.4 %psum.31 = f32[]{:T(128)} all-reduce(f32[]{:T(128)} %get-tuple-element.101), channel_id=1, replica_groups=mesh['lat'=4,'lon'=32] {'lat','lon'}, use_global_device_ids=true, to_apply=%region_13.14 | all-reduce | flops 1 | bytes 8 | tf_op jit(solution)/shard_map/psum | solution.py:207
  (188 shorter events, 105.5 us)
Async XLA Ops:
  7.2 24.0 %copy-start = (bf16[512,2048]{1,0:T(8,128)(2,1)S(1)}, bf16[512,2048]{1,0:T(8,128)(2,1)}, u32[]{:S(2)}) copy-start(bf16[512,2048]{1,0:T(8,128)(2,1)} %param.20) | copy-start | bytes 6291460
  7.2 23.1 %copy-start.12 = (bf16[512,128]{1,0:T(8,128)(2,1)S(1)}, bf16[512,128]{1,0:T(8,128)(2,1)}, u32[]{:S(2)}) copy-start(bf16[512,128]{1,0:T(8,128)(2,1)} %param.22) | copy-start | bytes 393220
  7.2 24.0 %copy-start.1 = (bf16[128,2048]{1,0:T(8,128)(2,1)S(1)}, bf16[128,2048]{1,0:T(8,128)(2,1)}, u32[]{:S(2)}) copy-start(bf16[128,2048]{1,0:T(8,128)(2,1)} %param.17) | copy-start | bytes 1572868
  7.2 162.5 %all-gather.10.cloned.1.call-start = ((), (), s32[]{:S(2)}) async-start(), calls=%async_computation.7 | async-start | bytes 4325376 | tf_op jit(solution)/shard_map/all_gather | solution.py:97
  7.9 320.3 %all-gather.12.cloned.1.call-start = ((), (), s32[]{:S(2)}) async-start(), calls=%async_computation.8 | async-start | bytes 4325376 | tf_op jit(solution)/shard_map/all_gather | solution.py:98
  10.1 3.0 copy-start.19
  11.4 1.7 copy-start.20
  13.1 10.8 all-to-all-start
  17.7 469.7 %all-gather.8.cloned.1.call-start = ((), (), s32[]{:S(2)}) async-start(), calls=%async_computation.6 | async-start | bytes 4325376 | tf_op jit(solution)/shard_map/all_gather | solution.py:120
  25.3 9.1 copy-start.3
  34.4 141.8 %copy-start.15 = (f32[128,512]{1,0:T(8,128)}, f32[128,512]{1,0:T(8,128)S(1)}, u32[]{:S(2)}) copy-start(f32[128,512]{1,0:T(8,128)S(1)} %fusion.17) | copy-start | bytes 786436
  35.4 625.0 %all-gather.14.cloned.1.call-start = ((), (), s32[]{:S(2)}) async-start(), calls=%async_computation.9 | async-start | bytes 4325376 | tf_op jit(solution)/shard_map/all_gather | solution.py:173
  328.2 98.9 %copy-start.18 = (bf16[128,512]{0,1:T(8,128)(2,1)S(1)}, bf16[128,512]{0,1:T(8,128)(2,1)}, u32[]{:S(2)}) copy-start(bf16[128,512]{0,1:T(8,128)(2,1)} %copy.81) | copy-start | bytes 393220
  493.8 7.7 copy-start.5
  493.8 7.7 copy-start.16
  493.8 9.0 copy-start.21
  502.8 373.3 %all-gather.16.cloned.1.call-start = ((), (), s32[]{:S(2)}) async-start(), calls=%async_computation.10 | async-start | bytes 4325376 | tf_op jit(solution)/shard_map/all_gather | solution.py:120
  666.8 7.7 copy-start.4
  666.8 8.7 copy-start.2
  674.5 4.0 copy-start.13
  720.7 461.3 %all-gather.18.cloned.1.call-start = ((), (), s32[]{:S(2)}) async-start(), calls=%async_computation.11 | async-start | bytes 4325376 | tf_op jit(solution)/shard_map/all_gather | solution.py:173
  882.5 7.7 copy-start.6
  882.5 7.7 copy-start.14
  1025.6 0.7 copy-start.8
  1028.3 368.5 %all-gather.20.cloned.1.call-start = ((), (), s32[]{:S(2)}) async-start(), calls=%async_computation.12 | async-start | bytes 4325376 | tf_op jit(solution)/shard_map/all_gather | solution.py:120
  1188.4 7.7 copy-start.9
  1403.2 7.7 copy-start.7
  1403.2 7.8 copy-start.10
  1403.2 7.8 copy-start.17
  1403.2 73.5 %copy-start.11 = (f32[128,512]{1,0:T(8,128)S(1)}, f32[128,512]{1,0:T(8,128)}, u32[]{:S(2)}) copy-start(f32[128,512]{1,0:T(8,128)} %get-tuple-element.100) | copy-start | bytes 786436
Sparse Core Ops, SparseCore 0:
  9.7 160.0 all-gather.9
  171.4 156.8 all-gather.11
  330.5 156.9 all-gather.7
  502.9 157.4 all-gather.13
  720.9 155.2 all-gather.15
  1028.4 153.5 all-gather.17
  1241.5 155.1 all-gather.19
where the time goes:
time: 1500 us; the launch traced here: 1480 us
  waiting for transfers between devices  940 us (63%)
  blocking collectives  320 us (21%)
  matrix products  103 us (7%)
  local copies, waits for them, and re-layouts  78.9 us (5%)
  between operations  18.7 us (1%)
  other arithmetic  18.3 us (1%)
    all_gather x3, waiting for transfers between devices, spread_back(): lax.all_gather(upward, 'lon', axis=0, tiled=True)  362 us
    all_gather x2, waiting for transfers between devices, per_device(): lax.all_gather(tangent_values, 'lon', axis=0, tiled=True)  287 us
    all_gather x1, waiting for transfers between devices, per_device(): lax.all_gather(key_states, 'lon', axis=0, tiled=True)  152 us
    all_gather x1, waiting for transfers between devices, per_device(): lax.all_gather(query_states, 'lon', axis=0, tiled=True)  134 us
    psum x2, blocking collectives, squares(): return lax.psum(jnp.sum(vector * vector), ('lat', 'lon'))  128 us
    all_gather x1, blocking collectives, per_device(): band_log = lax.all_gather(log_local, 'lon', axis=1, tiled=True)  81 us
    psum x1, blocking collectives, per_device(): lax.psum(jnp.sum(direction * applied), ('lat', 'lon'))  63.4 us
  transfers between devices with their start and end apart: 8, of which 8 were waited for; matrix products, arithmetic and copies ran while one was open for 4% of the time, Pallas kernels for 0%

commit v1 on v0

v1 whole, which is shorter than its diff:
```python
import math

import jax
import jax.numpy as jnp
from jax import lax
from jax.experimental import pallas as pl
from jax.experimental.pallas import tpu as pltpu
from jax.sharding import PartitionSpec as P

D = 512
HEADS = 8
HEAD_DIM = 64
FF = 2048
CHANNELS = 128
STENCIL = 4
TOK = 128
SLOTS = 128
N_LAT = 4
GROUP = 16
HALF = GROUP * TOK
SCORE_ROWS = 256
SCORE_SCALE = math.log2(math.e) / math.sqrt(HEAD_DIM)

MESH = pl.DeviceIdType.MESH
F32 = jnp.float32
BF16 = jnp.bfloat16
HIGHEST = lax.Precision.HIGHEST

KEYS, QUERIES, UP0, BACK0, VAL1, ATT1, UP1, BACK1, VAL2, ATT2, UP2, BACK2 = range(12)
STENCILS, ERRORS, STATS, SUMS = 12, 13, 14, 15
N_SUMS = 3
N_SEM = SUMS + 3 * N_SUMS


def mm(a, b):
    return jnp.dot(a, b, preferred_element_type=F32)


def contract(a, b, dim_a, dim_b, precision=None):
    return lax.dot_general(
        a, b, (((dim_a,), (dim_b,)), ((), ())), precision=precision, preferred_element_type=F32
    )


def fold(x):
    rows = jnp.sum(x, axis=0, keepdims=True)
    total = rows[:, 0:128]
    for c in range(128, x.shape[1], 128):
        total = total + rows[:, c : c + 128]
    return total


def kernel(
    query_ref,
    key_ref,
    slope_ref,
    w_value_ref,
    w_out_ref,
    w_up_ref,
    w_down_ref,
    w_obs_ref,
    cells_ref,
    weights_ref,
    count_ref,
    innov_ref,
    prec_ref,
    sol_ref,
    res_ref,
    arrived,
    blocks,
    parts,
    mix,
    stat_mine,
    stat_other,
    scale_ref,
    slope_t,
    st_stage,
    st_arrived,
    er_stage,
    er_arrived,
    sum_stage,
    sum_lat,
    sum_plane,
    sum_pair,
    send,
    recv,
):
    lat = lax.axis_index("lat")
    lon = lax.axis_index("lon")
    x, y, z = lax.div(lon, 8), lax.rem(lax.div(lon, 4), 2), lax.rem(lon, 4)
    i_half = lax.div(x, 2)
    head = lax.rem(x, 2) * 4 + z
    plane_me = x * 4 + z
    slab_me = lon - i_half * GROUP
    pair_lon = lon + 4 - 8 * y

    def plane_lon(t):
        return lax.div(t, 4) * 8 + y * 4 + lax.rem(t, 4)

    def plane_head(t):
        return lax.rem(lax.div(t, 4), 2) * 4 + lax.rem(t, 4)

    def slab_lon(t):
        return i_half * GROUP + t

    def slab_head(t):
        return lax.div(t, 8) * 4 + lax.rem(t, 4)

    def others(me, body):
        def one(k, carry):
            body(lax.rem(me + k, GROUP))
            return carry

        lax.fori_loop(1, GROUP, one, 0)

    def push(src, dst, sem, target):
        pltpu.make_async_remote_copy(
            src_ref=src,
            dst_ref=dst,
            send_sem=send.at[sem],
            recv_sem=recv.at[sem],
            device_id=target,
            device_id_type=MESH,
        ).start()

    def drain(ref, sem):
        pltpu.make_async_copy(ref, ref, sem).wait()

    def scatter_plane(e):
        others(
            plane_me,
            lambda t: push(
                blocks.at[e, plane_head(t)], arrived.at[e, plane_me], e, {"lon": plane_lon(t)}
            ),
        )
        arrived[e, plane_me] = blocks[e, head]

    def scatter_slab(e):
        others(
            slab_me,
            lambda t: push(
                blocks.at[e, slab_head(t)], arrived.at[e, slab_me], e, {"lon": slab_lon(t)}
            ),
        )
        arrived[e, slab_me] = blocks[e, head]

    def return_plane(e, p):
        slot = i_half * HEADS + head
        others(
            plane_me,
            lambda t: push(parts.at[p, t], arrived.at[e, slot], e, {"lon": plane_lon(t)}),
        )
        arrived[e, slot] = parts[p, plane_me]

    def return_slab(e, p):
        slot = y * HEADS + head
        others(
            slab_me,
            lambda t: push(parts.at[p, t], arrived.at[e, slot], e, {"lon": slab_lon(t)}),
        )
        arrived[e, slot] = parts[p, slab_me]

    def wait_group(e):
        drain(arrived.at[e, pl.ds(0, GROUP - 1)], recv.at[e])

    def wide(e):
        return jnp.concatenate([arrived[e, t] for t in range(GROUP)], axis=1)

    def joined(e):
        total = arrived[e, 0:HEADS].astype(F32) + arrived[e, HEADS:GROUP].astype(F32)
        return total.reshape(D, TOK)

    def put_blocks(e, matrix):
        blocks[e] = matrix.reshape(HEADS, HEAD_DIM, TOK)

    def put_parts(p, matrix):
        for t in range(GROUP):
            parts[p, t] = matrix[:, t * TOK : (t + 1) * TOK].astype(BF16)

    def sum_start(n, rows):
        row = lax.broadcasted_iota(jnp.int32, (8, 128), 0)
        tile = jnp.zeros((8, 128), F32)
        for r, values in enumerate(rows):
            tile = jnp.where(row == r, values, tile)
        sum_stage[n, 0] = tile
        sum_lat[n, lat] = tile

        def one(k, carry):
            push(
                sum_stage.at[n, 0],
                sum_lat.at[n, lat],
                SUMS + 3 * n,
                {"lat": lax.rem(lat + k, N_LAT)},
            )
            return carry

        lax.fori_loop(1, N_LAT, one, 0)

    def sum_middle(n):
        drain(sum_lat.at[n, pl.ds(0, N_LAT - 1)], recv.at[SUMS + 3 * n])
        tile = jnp.sum(sum_lat[n], axis=0)
        sum_stage[n, 1] = tile
        sum_plane[n, plane_me] = tile
        others(
            plane_me,
            lambda t: push(
                sum_stage.at[n, 1],
                sum_plane.at[n, plane_me],
                SUMS + 3 * n + 1,
                {"lon": plane_lon(t)},
            ),
        )

    def sum_last(n):
        drain(sum_plane.at[n, pl.ds(0, GROUP - 1)], recv.at[SUMS + 3 * n + 1])
        tile = jnp.sum(sum_plane[n], axis=0)
        sum_stage[n, 2] = tile
        push(sum_stage.at[n, 2], sum_pair.at[n], SUMS + 3 * n + 2, {"lon": pair_lon})

    def sum_end(n, count):
        drain(sum_pair.at[n], recv.at[SUMS + 3 * n + 2])
        tile = sum_stage[n, 2] + sum_pair[n]
        return [jnp.sum(tile[r : r + 1], axis=1, keepdims=True) for r in range(count)]

    barrier = pltpu.get_barrier_semaphore()

    def greet(target):
        pl.semaphore_signal(barrier, inc=1, device_id=target, device_id_type=MESH)

    others(plane_me, lambda t: greet({"lon": plane_lon(t)}))

    def greet_slab(k, carry):
        greet({"lon": i_half * GROUP + lax.div(k, 4) * 8 + (1 - y) * 4 + lax.rem(k, 4)})
        return carry

    lax.fori_loop(0, 8, greet_slab, 0)

    def greet_lat(k, carry):
        greet({"lat": lax.rem(lat + k, N_LAT)})
        return carry

    lax.fori_loop(1, N_LAT, greet_lat, 0)

    put_blocks(KEYS, key_ref[...].astype(F32).T.astype(BF16))
    put_blocks(QUERIES, query_ref[...].astype(F32).T.astype(BF16))
    prec_t = jnp.broadcast_to(prec_ref[...], (128, CHANNELS)).T
    lane = lax.broadcasted_iota(jnp.int32, (STENCIL, SLOTS), 1)
    for d in range(N_LAT):
        st_stage[d, 0:STENCIL] = cells_ref[0, 0, :, d, :].astype(F32)
        st_stage[d, STENCIL : 2 * STENCIL] = jnp.where(
            lane < count_ref[0, 0, d], weights_ref[0, 0, :, d, :], 0.0
        )
        er_stage[d] = (innov_ref[0, 0, :, d, :] * prec_t).astype(BF16)

    pl.semaphore_wait(barrier, GROUP - 1 + 8 + N_LAT - 1)

    def send_lat(k, carry):
        p = lax.rem(lat + k, N_LAT)
        push(st_stage.at[p], st_arrived.at[lat], STENCILS, {"lat": p})
        push(er_stage.at[p], er_arrived.at[lat], ERRORS, {"lat": p})
        return carry

    lax.fori_loop(1, N_LAT, send_lat, 0)
    st_arrived[lat] = st_stage[lat]
    er_arrived[lat] = er_stage[lat]
    scatter_plane(KEYS)
    scatter_slab(QUERIES)

    slope_t[...] = slope_ref[...].astype(F32).T.astype(BF16)

    drain(st_arrived.at[pl.ds(0, N_LAT - 1)], recv.at[STENCILS])
    token = lax.broadcasted_iota(jnp.int32, (TOK, SLOTS), 0).astype(F32)
    columns = []
    for a in range(N_LAT):
        rows = st_arrived[a]
        total = jnp.zeros((TOK, SLOTS), F32)
        for k in range(STENCIL):
            total = total + jnp.where(
                token == rows[k : k + 1], rows[STENCIL + k : STENCIL + k + 1], 0.0
            )
        columns.append(total)
    operator = jnp.concatenate(columns, axis=1)
    gram = contract(operator, operator, 1, 1, HIGHEST)
    drain(er_arrived.at[pl.ds(0, N_LAT - 1)], recv.at[ERRORS])
    errors = jnp.concatenate([er_arrived[a] for a in range(N_LAT)], axis=1).astype(F32)

    def adjoint_out(grad_t, e):
        g = mm(w_obs_ref[...], grad_t.astype(BF16))
        back = (mm(w_down_ref[...], g.astype(BF16)) * slope_t[...].astype(F32)).astype(BF16)
        middle = g + mm(w_up_ref[...], back)
        put_blocks(e, mm(w_out_ref[...], middle.astype(BF16)).astype(BF16))
        scatter_slab(e)
        return middle

    def adjoint_mix(e, p):
        upward = (wide(e).astype(F32) * scale_ref[...]).astype(BF16)
        put_parts(p, mm(upward, mix[...]))

    def adjoint_in(middle, e):
        wait_group(e)
        return (middle + mm(w_value_ref[...], joined(e).astype(BF16))).T

    def tangent_out(v, e):
        values = mm(v.astype(BF16), w_value_ref[...])
        put_blocks(e, values.T.astype(BF16))
        scatter_plane(e)

    def tangent_mix(e, p):
        put_parts(p, contract(wide(e), mix[...], 1, 1) * scale_ref[...])

    def tangent_in(v, attended):
        after = v + mm(attended, w_out_ref[...])
        hidden = (mm(after.astype(BF16), w_up_ref[...]) * slope_ref[...].astype(F32)).astype(BF16)
        y_field = after + mm(hidden, w_down_ref[...])
        field = mm(y_field.astype(BF16), w_obs_ref[...])
        grad_t = contract(field, gram, 0, 0, HIGHEST) * prec_t
        return field, grad_t

    middle = adjoint_out(contract(errors, operator, 1, 1, HIGHEST), UP0)

    wait_group(KEYS)
    wait_group(QUERIES)
    stat_lane = lax.broadcasted_iota(jnp.int32, (SCORE_ROWS, 128), 1)

    def score_rows(c, carry):
        query = jnp.concatenate([arrived[QUERIES, 2 * c], arrived[QUERIES, 2 * c + 1]], axis=1)
        scores = contract(query, wide(KEYS), 0, 0) * SCORE_SCALE
        top = jnp.max(scores, axis=1, keepdims=True)
        raised = jnp.exp2(scores - top)
        total = jnp.sum(raised, axis=1, keepdims=True)
        start = pl.multiple_of(c * SCORE_ROWS, SCORE_ROWS)
        mix[pl.ds(start, SCORE_ROWS), :] = raised.astype(BF16)
        stat = jnp.where(stat_lane == 0, top, total).T
        stat_mine[:, pl.ds(start, SCORE_ROWS)] = stat[0:8]
        return carry

    lax.fori_loop(0, HALF // SCORE_ROWS, score_rows, 0)
    push(stat_mine, stat_other, STATS, {"lon": pair_lon})
    wait_group(UP0)
    drain(stat_other, recv.at[STATS])
    top_mine, top_other = stat_mine[0:1], stat_other[0:1]
    top = jnp.maximum(top_mine, top_other)
    mine = jnp.exp2(top_mine - top)
    scale_ref[...] = mine / (
        stat_mine[1:2] * mine + stat_other[1:2] * jnp.exp2(top_other - top)
    )

    adjoint_mix(UP0, 0)
    return_plane(BACK0, 0)
    r1 = adjoint_in(middle, BACK0)

    tangent_out(r1, VAL1)
    rr1 = fold(r1 * r1)
    wait_group(VAL1)
    tangent_mix(VAL1, 1)
    return_slab(ATT1, 1)
    wait_group(ATT1)
    attended1 = joined(ATT1).T
    field, grad_t = tangent_in(r1, attended1.astype(BF16))
    sum_start(0, [rr1, fold(field * grad_t.T)])
    middle = adjoint_out(grad_t, UP1)
    sum_middle(0)
    wait_group(UP1)
    adjoint_mix(UP1, 2)
    return_plane(BACK1, 2)
    sum_last(0)
    applied = r1 + adjoint_in(middle, BACK1)
    norm1, seen1 = sum_end(0, 2)
    step1 = norm1 / (norm1 + seen1)
    r2 = r1 - step1 * applied

    tangent_out(r2, VAL2)
    sum_start(1, [fold(r2 * r2)])
    wait_group(VAL2)
    sum_middle(1)
    tangent_mix(VAL2, 3)
    return_slab(ATT2, 3)
    sum_last(1)
    wait_group(ATT2)
    (norm2,) = sum_end(1, 1)
    beta = norm2 / norm1
    d2 = r2 + beta * r1
    attended2 = joined(ATT2).T + beta * attended1
    field, grad_t = tangent_in(d2, attended2.astype(BF16))
    sum_start(2, [fold(d2 * d2), fold(field * grad_t.T)])
    middle = adjoint_out(grad_t, UP2)
    sum_middle(2)
    wait_group(UP2)
    adjoint_mix(UP2, 4)
    return_plane(BACK2, 4)
    sum_last(2)
    applied = d2 + adjoint_in(middle, BACK2)
    squared2, seen2 = sum_end(2, 2)
    step2 = norm2 / (squared2 + seen2)
    sol_ref[...] = step1 * r1 + step2 * d2
    res_ref[...] = r2 - step2 * applied

    for e in range(12):
        drain(arrived.at[e, pl.ds(0, GROUP - 1)], send.at[e])
    drain(st_stage.at[pl.ds(0, N_LAT - 1)], send.at[STENCILS])
    drain(er_stage.at[pl.ds(0, N_LAT - 1)], send.at[ERRORS])
    drain(stat_mine, send.at[STATS])
    for n in range(N_SUMS):
        drain(sum_lat.at[n, pl.ds(0, N_LAT - 1)], send.at[SUMS + 3 * n])
        drain(sum_plane.at[n, pl.ds(0, GROUP - 1)], send.at[SUMS + 3 * n + 1])
        drain(sum_pair.at[n], send.at[SUMS + 3 * n + 2])


def per_device(*args):
    args = list(args)
    args[12] = args[12].reshape(1, CHANNELS)
    vmem = pl.BlockSpec(memory_space=pltpu.VMEM)
    in_specs = [vmem] * 13
    in_specs[10] = pl.BlockSpec(memory_space=pltpu.SMEM)
    return pl.pallas_call(
        kernel,
        out_shape=(jax.ShapeDtypeStruct((TOK, D), F32),) * 2,
        in_specs=in_specs,
        out_specs=(vmem, vmem),
        scratch_shapes=[
            pltpu.VMEM((12, GROUP, HEAD_DIM, TOK), BF16),
            pltpu.VMEM((12, HEADS, HEAD_DIM, TOK), BF16),
            pltpu.VMEM((5, GROUP, HEAD_DIM, TOK), BF16),
            pltpu.VMEM((HALF, HALF), BF16),
            pltpu.VMEM((8, HALF), F32),
            pltpu.VMEM((8, HALF), F32),
            pltpu.VMEM((1, HALF), F32),
            pltpu.VMEM((FF, TOK), BF16),
            pltpu.VMEM((N_LAT, 2 * STENCIL, SLOTS), F32),
            pltpu.VMEM((N_LAT, 2 * STENCIL, SLOTS), F32),
            pltpu.VMEM((N_LAT, CHANNELS, SLOTS), BF16),
            pltpu.VMEM((N_LAT, CHANNELS, SLOTS), BF16),
            pltpu.VMEM((N_SUMS, 3, 8, 128), F32),
            pltpu.VMEM((N_SUMS, N_LAT, 8, 128), F32),
            pltpu.VMEM((N_SUMS, GROUP, 8, 128), F32),
            pltpu.VMEM((N_SUMS, 8, 128), F32),
            pltpu.SemaphoreType.DMA((N_SEM,)),
            pltpu.SemaphoreType.DMA((N_SEM,)),
        ],
        compiler_params=pltpu.CompilerParams(
            collective_id=0, has_side_effects=True, vmem_limit_bytes=56 * 1024 * 1024
        ),
    )(*args)


def solution(mesh):
    in_specs = (
        P(("lat", "lon"), None),
        P(("lat", "lon"), None),
        P(("lat", "lon"), None),
        P(),
        P(),
        P(),
        P(),
        P(),
        P("lat", "lon", None, None, None),
        P("lat", "lon", None, None, None),
        P("lat", "lon", None),
        P("lat", "lon", None, None, None),
        P(),
    )
    out_specs = (P(("lat", "lon"), None), P(("lat", "lon"), None))
    return jax.shard_map(
        per_device, mesh=mesh, in_specs=in_specs, out_specs=out_specs, check_vma=False
    )
```

time: 1500 us -> 106 us (0.07); the launches traced: 1480 us -> 106 us
  waiting for transfers between devices: 940 us -> 0 us
  blocking collectives: 320 us -> 0 us
  matrix products: 103 us -> 0 us
  Pallas kernels: 0 us -> 102 us
  local copies, waits for them, and re-layouts: 78.9 us -> 3.34 us
  other arithmetic: 18.3 us -> 0 us
  between operations: 18.7 us -> 0.64 us
    all_gather x7 -> x0, waiting for transfers between devices: 935 us -> none  [the longest x3 362 us: spread_back(): lax.all_gather(upward, 'lon', axis=0, tiled=True)]
    psum x3 -> x0, blocking collectives: 192 us -> none  [the longest x2 128 us: squares(): return lax.psum(jnp.sum(vector * vector), ('lat', 'lon'))]
    dot_general x40 -> x0, matrix products: 103 us -> none  [the longest x3 23.1 us: mix_back(): jnp.einsum('hts,shd->thd', frozen, with_heads(upward_part), preferred_ele...]
    pallas_call x0 -> x1, Pallas kernels: none -> 102 us  [per_device(): pl.pallas_call(kernel, out_shape=(jax.ShapeDtypeStruct((TOK, D), F32),) *...]
    all_gather x1 -> x0, blocking collectives: 81 us -> none  [per_device(): band_log = lax.all_gather(log_local, 'lon', axis=1, tiled=True)]
    all_to_all x5 -> x0, blocking collectives: 47 us -> none  [the longest x2 19.9 us: per_device(): lax.all_to_all(forward_values(operator_matrix(observe_arrived, tok_rows),...]
    all_gather x7 -> x0, local copies, waits for them, and re-layouts: 45 us -> none  [the longest x3 19.3 us: spread_back(): lax.all_gather(upward, 'lon', axis=0, tiled=True)]
  transfers between devices with their start and end apart: 8 -> 0, of which waited for: 8 -> 0; matrix products, arithmetic and copies ran while one was open for 4% -> 0% of each run, Pallas kernels for 0% -> 0%
where the time goes in v1:
time: 106 us
  Pallas kernels  102 us (96%)
  local copies, waits for them, and re-layouts  3.34 us (3%)
    pallas_call x1, Pallas kernels, per_device(): pl.pallas_call(kernel, out_shape=(jax.ShapeDtypeStruct((TOK, D), F32),) *...  102 us
    unnamed x2, local copies, waits for them, and re-layouts  3.34 us

profile of v1, /device:TPU:0, one launch (start us, length us, event | category | flops | bytes accessed | tf_op | source)
XLA Modules:
  0.0 106.0 jit_solution(12807746809079012222)
XLA Ops:
  0.6 102.0 %shard_map.140 = (f32[128,512]{1,0:T(8,128)}, f32[128,512]{1,0:T(8,128)}) custom-call(bf16[128,512]{1,0:T(8,128)(2,1)} %query_ref.1, bf16[128,512]{1,0:T(8,128)(2,1)} %key_ref.1, bf16[128,2048]{1,0:T(8,128)(2,1)} %slope_ref.1, bf16[512,512]{1,0:T(8,128)(2,1)} %w_value_ref.1, bf16[512,512]{1,0:T(8,128)(2,1)} %w_out_ref.1, bf16[512,2048]{1,0:T(8,128)(2,1)} %w_up_ref.1, ...), custom_call_target="tpu_custom_call" | custom-call | tf_op jit(solution)/shard_map/pallas_call | solution.py:415
  102.7 1.7 %copy.17 = f32[128,512]{1,0:T(8,128)} copy(f32[128,512]{1,0:T(8,128)} %get-tuple-element.4) | data formatting | bytes 524288
  104.4 1.7 %copy.18 = f32[128,512]{1,0:T(8,128)} copy(f32[128,512]{1,0:T(8,128)} %get-tuple-element.5) | data formatting | bytes 524288

commit v2 on v1

v2 whole, which is shorter than its diff:
```python
import math

import jax
import jax.numpy as jnp
from jax import lax
from jax.experimental import pallas as pl
from jax.experimental.pallas import tpu as pltpu
from jax.sharding import PartitionSpec as P

D = 512
HEADS = 8
HEAD_DIM = 64
FF = 2048
CHANNELS = 128
STENCIL = 4
TOK = 128
SLOTS = 128
N_LAT = 4
GROUP = 16
HALF = GROUP * TOK
SCORE_SCALE = math.log2(math.e) / math.sqrt(HEAD_DIM)

MESH = pl.DeviceIdType.MESH
F32 = jnp.float32
BF16 = jnp.bfloat16
HIGHEST = lax.Precision.HIGHEST

KEYS, QUERIES, UP0, BACK0, VAL1, ATT1, UP1, BACK1, VAL2, ATT2, UP2, BACK2 = range(12)
N_EXCHANGES = 12
STENCILS, ERRORS, STATS, SUMS = 0, 1, 2, 4
N_SUMS = 3
N_OTHER = SUMS + 3 * N_SUMS


def hops(offset):
    dx, dy, dz = offset
    return dx + dy + min(dz, 4 - dz)


GROUP_OFFSETS = sorted(
    [(dx, dy, dz) for dx in (1, 0) for dy in (1, 0) for dz in (2, 1, 3, 0) if (dx, dy, dz) != (0, 0, 0)],
    key=hops,
    reverse=True,
)


def mm(a, b):
    return jnp.dot(a, b, preferred_element_type=F32)


def contract(a, b, dim_a, dim_b, precision=None):
    return lax.dot_general(
        a, b, (((dim_a,), (dim_b,)), ((), ())), precision=precision, preferred_element_type=F32
    )


def total_of(x):
    return jnp.sum(jnp.sum(x, axis=0, keepdims=True), axis=1, keepdims=True)


def kernel(
    query_hbm,
    key_hbm,
    slope_hbm,
    w_value_hbm,
    w_out_hbm,
    w_up_hbm,
    w_down_hbm,
    w_obs_hbm,
    cells_hbm,
    weights_hbm,
    count_ref,
    innov_hbm,
    prec_hbm,
    sol_ref,
    res_ref,
    query_ref,
    key_ref,
    slope_ref,
    w_value_ref,
    w_out_ref,
    w_up_ref,
    w_down_ref,
    w_obs_ref,
    cells_ref,
    weights_ref,
    innov_ref,
    prec_ref,
    arrived,
    blocks,
    parts,
    half_sum,
    mix,
    stat_mine,
    stat_other,
    scale_ref,
    slope_t,
    st_stage,
    st_arrived,
    er_stage,
    er_arrived,
    sum_stage,
    sum_lat,
    sum_group,
    sum_pair,
    load,
    send,
    recv,
    other_send,
    other_recv,
):
    loads = {}
    for n, (src, dst) in enumerate(
        [
            (key_hbm, key_ref),
            (query_hbm, query_ref),
            (prec_hbm, prec_ref),
            (cells_hbm, cells_ref),
            (weights_hbm, weights_ref),
            (innov_hbm, innov_ref),
            (slope_hbm, slope_ref),
            (w_obs_hbm, w_obs_ref),
            (w_down_hbm, w_down_ref),
            (w_up_hbm, w_up_ref),
            (w_out_hbm, w_out_ref),
            (w_value_hbm, w_value_ref),
        ]
    ):
        loads[id(dst)] = pltpu.make_async_copy(src, dst, load.at[n])
        loads[id(dst)].start()

    lat = lax.axis_index("lat")
    lon = lax.axis_index("lon")
    x, y, z = lax.div(lon, 8), lax.rem(lax.div(lon, 4), 2), lax.rem(lon, 4)
    row = y * 4 + z
    bit_i = lax.rem(x, 2)
    bit_j = 1 - bit_i
    mate_i = x + 1 - 2 * bit_i
    mate_j = lax.rem(x + 5 - 2 * bit_j, 4)
    slot_i = bit_i * 8 + row
    slot_j = bit_j * 8 + row
    rows_by = {
        (dy, dz): (y + dy - 2 * y * dy) * 4 + (lax.rem(z + dz, 4) if dz else z)
        for dy in range(2)
        for dz in range(4)
    }

    def member(by_i, offset):
        dx, dy, dz = offset
        bit = bit_i if by_i else bit_j
        place = x if dx == 0 else (mate_i if by_i else mate_j)
        there = rows_by[dy, dz]
        return (bit + dx - 2 * bit * dx) * 8 + there, place * 8 + there

    def remote(src, dst, send_sem, recv_sem, target):
        pltpu.make_async_remote_copy(
            src_ref=src,
            dst_ref=dst,
            send_sem=send_sem,
            recv_sem=recv_sem,
            device_id=target,
            device_id_type=MESH,
        ).start()

    def push(src, dst, n, target):
        remote(src, dst, other_send.at[n], other_recv.at[n], target)

    def drain(ref, sem):
        pltpu.make_async_copy(ref, ref, sem).wait()

    def scatter(e, by_i, matrix):
        blocks[e] = matrix.reshape(HEADS, HEAD_DIM, TOK)
        me = slot_i if by_i else slot_j
        for offset in GROUP_OFFSETS:
            slot, place = member(by_i, offset)
            remote(
                blocks.at[e, rows_by[offset[1:]]],
                arrived.at[e, me],
                send.at[e],
                recv.at[e, offset[0]],
                {"lon": place},
            )
        arrived[e, me] = blocks[e, row]

    def send_part(e, p, by_i, offset, block):
        me = slot_i if by_i else slot_j
        if offset == (0, 0, 0):
            arrived[e, me] = block
            return
        slot, place = member(by_i, offset)
        parts[p, slot] = block
        remote(
            parts.at[p, slot], arrived.at[e, me], send.at[e], recv.at[e, offset[0]], {"lon": place}
        )

    def wait_near(e):
        drain(arrived.at[e, pl.ds(0, HEADS - 1)], recv.at[e, 0])

    def wait_far(e):
        drain(arrived.at[e, pl.ds(0, HEADS)], recv.at[e, 1])

    def half(e, bit):
        return jnp.concatenate([arrived[e, bit * HEADS + t] for t in range(HEADS)], axis=1)

    def joined(e):
        wait_near(e)
        wait_far(e)
        total = arrived[e, 0:HEADS].astype(F32) + arrived[e, HEADS:GROUP].astype(F32)
        return total.reshape(D, TOK)

    def span(index, size):
        return pl.ds(pl.multiple_of(index * size, size), size)

    def quarters(by_i, one):
        bit = bit_i if by_i else bit_j
        for dx, dy in ((1, 1), (1, 0), (0, 1), (0, 0)):
            quarter = (bit + dx - 2 * bit * dx) * 2 + (y + dy - 2 * y * dy)
            one(quarter, dx, dy)

    lane = lax.broadcasted_iota(jnp.int32, (1, 128), 1)

    def sum_start(n, values):
        tile = jnp.zeros((1, 128), F32)
        for r, value in enumerate(values):
            tile = jnp.where(lane == r, value, tile)
        sum_stage[n, 0] = tile
        sum_lat[n, lat] = tile
        for k in range(1, N_LAT):
            push(
                sum_stage.at[n, 0],
                sum_lat.at[n, lat],
                SUMS + 3 * n,
                {"lat": lax.rem(lat + k, N_LAT)},
            )

    def sum_middle(n):
        drain(sum_lat.at[n, pl.ds(0, N_LAT - 1)], other_recv.at[SUMS + 3 * n])
        tile = jnp.sum(sum_lat[n], axis=0)
        sum_stage[n, 1] = tile
        sum_group[n, slot_i] = tile
        for offset in GROUP_OFFSETS:
            push(
                sum_stage.at[n, 1],
                sum_group.at[n, slot_i],
                SUMS + 3 * n + 1,
                {"lon": member(True, offset)[1]},
            )

    def sum_last(n):
        drain(sum_group.at[n, pl.ds(0, GROUP - 1)], other_recv.at[SUMS + 3 * n + 1])
        sum_stage[n, 2] = jnp.sum(sum_group[n], axis=0)
        push(
            sum_stage.at[n, 2],
            sum_pair.at[n],
            SUMS + 3 * n + 2,
            {"lon": mate_j * 8 + row},
        )

    def sum_end(n, count):
        drain(sum_pair.at[n], other_recv.at[SUMS + 3 * n + 2])
        tile = sum_stage[n, 2] + sum_pair[n]
        return [
            jnp.sum(jnp.where(lane == r, tile, 0.0), axis=1, keepdims=True) for r in range(count)
        ]

    barrier = pltpu.get_barrier_semaphore()

    def greet(target):
        pl.semaphore_signal(barrier, inc=1, device_id=target, device_id_type=MESH)

    for offset in GROUP_OFFSETS:
        greet({"lon": member(True, offset)[1]})
    for offset in GROUP_OFFSETS:
        if offset[0] == 1:
            greet({"lon": member(False, offset)[1]})
    for k in range(1, N_LAT):
        greet({"lat": lax.rem(lat + k, N_LAT)})

    loads[id(key_ref)].wait()
    keys_t = key_ref[...].astype(F32).T.astype(BF16)
    loads[id(query_ref)].wait()
    queries_t = query_ref[...].astype(F32).T.astype(BF16)
    loads[id(prec_ref)].wait()
    prec_t = jnp.broadcast_to(prec_ref[...], (128, CHANNELS)).T
    loads[id(cells_ref)].wait()
    loads[id(weights_ref)].wait()
    loads[id(innov_ref)].wait()
    slot_lane = lax.broadcasted_iota(jnp.int32, (STENCIL, SLOTS), 1)
    for d in range(N_LAT):
        st_stage[d, 0:STENCIL] = cells_ref[0, 0, :, d, :].astype(F32)
        st_stage[d, STENCIL : 2 * STENCIL] = jnp.where(
            slot_lane < count_ref[0, 0, d], weights_ref[0, 0, :, d, :], 0.0
        )
        er_stage[d] = (innov_ref[0, 0, :, d, :] * prec_t).astype(BF16)

    pl.semaphore_wait(barrier, GROUP - 1 + HEADS + N_LAT - 1)

    scatter(KEYS, False, keys_t)
    for k in range(1, N_LAT):
        p = lax.rem(lat + k, N_LAT)
        push(st_stage.at[p], st_arrived.at[lat], STENCILS, {"lat": p})
        push(er_stage.at[p], er_arrived.at[lat], ERRORS, {"lat": p})
    st_arrived[lat] = st_stage[lat]
    er_arrived[lat] = er_stage[lat]
    scatter(QUERIES, True, queries_t)

    loads[id(slope_ref)].wait()
    slope_t[...] = slope_ref[...].astype(F32).T.astype(BF16)

    drain(st_arrived.at[pl.ds(0, N_LAT - 1)], other_recv.at[STENCILS])
    token = lax.broadcasted_iota(jnp.int32, (TOK, SLOTS), 0).astype(F32)
    columns = []
    for a in range(N_LAT):
        rows = st_arrived[a]
        total = jnp.zeros((TOK, SLOTS), F32)
        for k in range(STENCIL):
            total = total + jnp.where(
                token == rows[k : k + 1], rows[STENCIL + k : STENCIL + k + 1], 0.0
            )
        columns.append(total)
    operator = jnp.concatenate(columns, axis=1)
    gram = contract(operator, operator, 1, 1, HIGHEST)
    drain(er_arrived.at[pl.ds(0, N_LAT - 1)], other_recv.at[ERRORS])
    errors = jnp.concatenate([er_arrived[a] for a in range(N_LAT)], axis=1).astype(F32)
    for ref in (w_obs_ref, w_down_ref, w_up_ref, w_out_ref, w_value_ref):
        loads[id(ref)].wait()

    def adjoint_out(grad_t, e):
        g = mm(w_obs_ref[...], grad_t.astype(BF16))
        back = (mm(w_down_ref[...], g.astype(BF16)) * slope_t[...].astype(F32)).astype(BF16)
        middle = g + mm(w_up_ref[...], back)
        scatter(e, True, mm(w_out_ref[...], middle.astype(BF16)).astype(BF16))
        return middle

    def adjoint_mix(e, back, p):
        wait_near(e)
        upward = (half(e, bit_i).astype(F32) * scale_ref[:, span(bit_i, HALF // 2)]).astype(BF16)
        half_sum[...] = mm(upward, mix[span(bit_i, HALF // 2), :])
        wait_far(e)
        rest = (half(e, bit_j).astype(F32) * scale_ref[:, span(bit_j, HALF // 2)]).astype(BF16)

        def one(quarter, dx, dy):
            cols = span(quarter, HALF // 4)
            half_sum[:, cols] += mm(rest, mix[span(bit_j, HALF // 2), cols])
            for dz in (2, 1, 3, 0):
                piece = half_sum[:, span(quarter * 4 + lax.rem(z + dz, 4), TOK)]
                send_part(back, p, False, (dx, dy, dz), piece.astype(BF16))

        quarters(False, one)

    def adjoint_in(middle, e):
        return (middle + mm(w_value_ref[...], joined(e).astype(BF16))).T

    def tangent_out(v, e):
        scatter(e, False, mm(v.astype(BF16), w_value_ref[...]).T.astype(BF16))

    def tangent_mix(e, back, p):
        wait_near(e)
        half_sum[...] = contract(half(e, bit_j), mix[:, span(bit_j, HALF // 2)], 1, 1)
        wait_far(e)
        rest = half(e, bit_i)

        def one(quarter, dx, dy):
            cols = span(quarter, HALF // 4)
            out = half_sum[:, cols] + contract(rest, mix[cols, span(bit_i, HALF // 2)], 1, 1)
            half_sum[:, cols] = out * scale_ref[:, cols]
            for dz in (2, 1, 3, 0):
                piece = half_sum[:, span(quarter * 4 + lax.rem(z + dz, 4), TOK)]
                send_part(back, p, True, (dx, dy, dz), piece.astype(BF16))

        quarters(True, one)

    def tangent_in(v, attended):
        after = v + mm(attended, w_out_ref[...])
        hidden = (mm(after.astype(BF16), w_up_ref[...]) * slope_ref[...].astype(F32)).astype(BF16)
        y_field = after + mm(hidden, w_down_ref[...])
        field = mm(y_field.astype(BF16), w_obs_ref[...])
        grad_t = contract(field, gram, 0, 0, HIGHEST) * prec_t
        return field, grad_t

    middle = adjoint_out(contract(errors, operator, 1, 1, HIGHEST), UP0)

    wait_near(KEYS)
    wait_far(KEYS)
    stat_lane = lax.broadcasted_iota(jnp.int32, (TOK, 128), 1)
    keys = jnp.concatenate([arrived[KEYS, t] for t in range(GROUP)], axis=1)
    keys = jnp.concatenate([keys, keys], axis=0)

    def score_rows(slot):
        scaled = arrived[QUERIES, slot].astype(F32) * SCORE_SCALE
        high = scaled.astype(BF16)
        low = (scaled - high.astype(F32)).astype(BF16)
        scores = contract(jnp.concatenate([high, low], axis=0), keys, 0, 0)
        top = jnp.max(scores, axis=1, keepdims=True)
        raised = jnp.exp2(scores - top)
        total = jnp.sum(raised, axis=1, keepdims=True)
        mix[span(slot, TOK), :] = raised.astype(BF16)
        stat = jnp.where(stat_lane == 0, top, total).T
        stat_mine[:, span(slot, TOK)] = stat[0:8]

    pair = {"lon": mate_i * 8 + row}

    def score_half(bit, sem):
        for t in range(HEADS):
            score_rows(bit * HEADS + t)
        place = span(bit, HALF // 2)
        push(stat_mine.at[:, place], stat_other.at[:, place], sem, pair)

    def set_scale(bit, sem):
        place = span(bit, HALF // 2)
        drain(stat_other.at[:, pl.ds(0, HALF // 2)], other_recv.at[sem])
        top_mine, top_other = stat_mine[0:1, place], stat_other[0:1, place]
        top = jnp.maximum(top_mine, top_other)
        mine = jnp.exp2(top_mine - top)
        scale_ref[:, place] = mine / (
            stat_mine[1:2, place] * mine + stat_other[1:2, place] * jnp.exp2(top_other - top)
        )

    wait_near(QUERIES)
    wait_far(QUERIES)
    score_half(0, STATS)
    score_half(1, STATS + 1)
    set_scale(0, STATS)
    set_scale(1, STATS + 1)

    adjoint_mix(UP0, BACK0, 0)
    r1 = adjoint_in(middle, BACK0)

    tangent_out(r1, VAL1)
    rr1 = total_of(r1 * r1)
    tangent_mix(VAL1, ATT1, 1)
    attended1 = joined(ATT1).T
    field, grad_t = tangent_in(r1, attended1.astype(BF16))
    sum_start(0, [rr1, total_of(field * grad_t.T)])
    middle = adjoint_out(grad_t, UP1)
    sum_middle(0)
    adjoint_mix(UP1, BACK1, 2)
    sum_last(0)
    applied = r1 + adjoint_in(middle, BACK1)
    norm1, seen1 = sum_end(0, 2)
    step1 = norm1 / (norm1 + seen1)
    r2 = r1 - step1 * applied

    tangent_out(r2, VAL2)
    sum_start(1, [total_of(r2 * r2)])
    sum_middle(1)
    tangent_mix(VAL2, ATT2, 3)
    sum_last(1)
    attended2 = joined(ATT2).T
    (norm2,) = sum_end(1, 1)
    beta = norm2 / norm1
    d2 = r2 + beta * r1
    attended2 = attended2 + beta * attended1
    field, grad_t = tangent_in(d2, attended2.astype(BF16))
    sum_start(2, [total_of(d2 * d2), total_of(field * grad_t.T)])
    middle = adjoint_out(grad_t, UP2)
    sum_middle(2)
    adjoint_mix(UP2, BACK2, 4)
    sum_last(2)
    applied = d2 + adjoint_in(middle, BACK2)
    squared2, seen2 = sum_end(2, 2)
    step2 = norm2 / (squared2 + seen2)
    sol_ref[...] = step1 * r1 + step2 * d2
    res_ref[...] = r2 - step2 * applied

    for e in range(N_EXCHANGES):
        drain(arrived.at[e, pl.ds(0, GROUP - 1)], send.at[e])
    drain(st_stage.at[pl.ds(0, N_LAT - 1)], other_send.at[STENCILS])
    drain(er_stage.at[pl.ds(0, N_LAT - 1)], other_send.at[ERRORS])
    for k in range(2):
        drain(stat_mine.at[:, pl.ds(0, HALF // 2)], other_send.at[STATS + k])
    for n in range(N_SUMS):
        drain(sum_lat.at[n, pl.ds(0, N_LAT - 1)], other_send.at[SUMS + 3 * n])
        drain(sum_group.at[n, pl.ds(0, GROUP - 1)], other_send.at[SUMS + 3 * n + 1])
        drain(sum_pair.at[n], other_send.at[SUMS + 3 * n + 2])


def per_device(*args):
    args = list(args)
    args[12] = args[12].reshape(1, CHANNELS)
    hbm = pl.BlockSpec(memory_space=pl.ANY)
    vmem = pl.BlockSpec(memory_space=pltpu.VMEM)
    in_specs = [hbm] * 13
    in_specs[10] = pl.BlockSpec(memory_space=pltpu.SMEM)
    return pl.pallas_call(
        kernel,
        out_shape=(jax.ShapeDtypeStruct((TOK, D), F32),) * 2,
        in_specs=in_specs,
        out_specs=(vmem, vmem),
        scratch_shapes=[
            *[pltpu.VMEM(a.shape, a.dtype) for n, a in enumerate(args) if n != 10],
            pltpu.VMEM((N_EXCHANGES, GROUP, HEAD_DIM, TOK), BF16),
            pltpu.VMEM((N_EXCHANGES, HEADS, HEAD_DIM, TOK), BF16),
            pltpu.VMEM((5, GROUP, HEAD_DIM, TOK), BF16),
            pltpu.VMEM((HEAD_DIM, HALF), F32),
            pltpu.VMEM((HALF, HALF), BF16),
            pltpu.VMEM((8, HALF), F32),
            pltpu.VMEM((8, HALF), F32),
            pltpu.VMEM((1, HALF), F32),
            pltpu.VMEM((FF, TOK), BF16),
            pltpu.VMEM((N_LAT, 2 * STENCIL, SLOTS), F32),
            pltpu.VMEM((N_LAT, 2 * STENCIL, SLOTS), F32),
            pltpu.VMEM((N_LAT, CHANNELS, SLOTS), BF16),
            pltpu.VMEM((N_LAT, CHANNELS, SLOTS), BF16),
            pltpu.VMEM((N_SUMS, 3, 1, 128), F32),
            pltpu.VMEM((N_SUMS, N_LAT, 1, 128), F32),
            pltpu.VMEM((N_SUMS, GROUP, 1, 128), F32),
            pltpu.VMEM((N_SUMS, 1, 128), F32),
            pltpu.SemaphoreType.DMA((12,)),
            pltpu.SemaphoreType.DMA((N_EXCHANGES,)),
            pltpu.SemaphoreType.DMA((N_EXCHANGES, 2)),
            pltpu.SemaphoreType.DMA((N_OTHER,)),
            pltpu.SemaphoreType.DMA((N_OTHER,)),
        ],
        compiler_params=pltpu.CompilerParams(
            collective_id=0, has_side_effects=True, vmem_limit_bytes=56 * 1024 * 1024
        ),
    )(*args)


def solution(mesh):
    in_specs = (
        P(("lat", "lon"), None),
        P(("lat", "lon"), None),
        P(("lat", "lon"), None),
        P(),
        P(),
        P(),
        P(),
        P(),
        P("lat", "lon", None, None, None),
        P("lat", "lon", None, None, None),
        P("lat", "lon", None),
        P("lat", "lon", None, None, None),
        P(),
    )
    out_specs = (P(("lat", "lon"), None), P(("lat", "lon"), None))
    return jax.shard_map(
        per_device, mesh=mesh, in_specs=in_specs, out_specs=out_specs, check_vma=False
    )
```

time: 106 us -> 97.6 us (0.921)
  Pallas kernels: 102 us -> 93.4 us
    pallas_call x1, Pallas kernels: 102 us -> 93.4 us  [per_device(): pl.pallas_call(kernel, out_shape=(jax.ShapeDtypeStruct((TOK, D), F32),) *...]
where the time goes in v2:
time: 97.6 us; the launch traced here: 97.4 us
  Pallas kernels  93.4 us (96%)
  local copies, waits for them, and re-layouts  3.34 us (3%)
    pallas_call x1, Pallas kernels, per_device(): pl.pallas_call(kernel, out_shape=(jax.ShapeDtypeStruct((TOK, D), F32),) *...  93.4 us
    unnamed x2, local copies, waits for them, and re-layouts  3.34 us

profile of v2, /device:TPU:0, one launch (start us, length us, event | category | flops | bytes accessed | tf_op | source)
XLA Modules:
  0.0 97.4 jit_solution(5523139250569765982)
XLA Ops:
  0.6 93.4 %shard_map.140 = (f32[128,512]{1,0:T(8,128)}, f32[128,512]{1,0:T(8,128)}) custom-call(bf16[128,512]{1,0:T(8,128)(2,1)} %query_hbm.1, bf16[128,512]{1,0:T(8,128)(2,1)} %key_hbm.1, bf16[128,2048]{1,0:T(8,128)(2,1)} %slope_hbm.1, bf16[512,512]{1,0:T(8,128)(2,1)} %w_value_hbm.1, bf16[512,512]{1,0:T(8,128)(2,1)} %w_out_hbm.1, bf16[512,2048]{1,0:T(8,128)(2,1)} %w_up_hbm.1, ...), custom_call_target="tpu_custom_call" | custom-call | tf_op jit(solution)/shard_map/pallas_call | solution.py:485
  94.1 1.7 %copy.17 = f32[128,512]{1,0:T(8,128)} copy(f32[128,512]{1,0:T(8,128)} %get-tuple-element.4) | data formatting | bytes 524288
  95.7 1.7 %copy.18 = f32[128,512]{1,0:T(8,128)} copy(f32[128,512]{1,0:T(8,128)} %get-tuple-element.5) | data formatting | bytes 524288

commit v3 on v2

--- a/solution.py
+++ b/solution.py
@@ -95,6 +95,11 @@
     stat_other,
     scale_ref,
     slope_t,
+    w_do,
+    w_oo,
+    w_ou,
+    w_value_t,
+    w_vv,
     st_stage,
     st_arrived,
     er_stage,
@@ -110,24 +115,13 @@
     other_recv,
 ):
     loads = {}
-    for n, (src, dst) in enumerate(
-        [
-            (key_hbm, key_ref),
-            (query_hbm, query_ref),
-            (prec_hbm, prec_ref),
-            (cells_hbm, cells_ref),
-            (weights_hbm, weights_ref),
-            (innov_hbm, innov_ref),
-            (slope_hbm, slope_ref),
-            (w_obs_hbm, w_obs_ref),
-            (w_down_hbm, w_down_ref),
-            (w_up_hbm, w_up_ref),
-            (w_out_hbm, w_out_ref),
-            (w_value_hbm, w_value_ref),
-        ]
-    ):
-        loads[id(dst)] = pltpu.make_async_copy(src, dst, load.at[n])
-        loads[id(dst)].start()
+
+    def start_loads(pairs):
+        for src, dst in pairs:
+            loads[id(dst)] = pltpu.make_async_copy(src, dst, load.at[len(loads)])
+            loads[id(dst)].start()
+
+    start_loads([(key_hbm, key_ref), (query_hbm, query_ref)])
 
     lat = lax.axis_index("lat")
     lon = lax.axis_index("lon")
@@ -137,8 +131,9 @@
     bit_j = 1 - bit_i
     mate_i = x + 1 - 2 * bit_i
     mate_j = lax.rem(x + 5 - 2 * bit_j, 4)
-    slot_i = bit_i * 8 + row
-    slot_j = bit_j * 8 + row
+    slot_i = y * 8 + bit_i * 4 + z
+    slot_j = y * 8 + bit_j * 4 + z
+    near, far = y, 1 - y
     rows_by = {
         (dy, dz): (y + dy - 2 * y * dy) * 4 + (lax.rem(z + dz, 4) if dz else z)
         for dy in range(2)
@@ -150,7 +145,8 @@
         bit = bit_i if by_i else bit_j
         place = x if dx == 0 else (mate_i if by_i else mate_j)
         there = rows_by[dy, dz]
-        return (bit + dx - 2 * bit * dx) * 8 + there, place * 8 + there
+        slot = (y + dy - 2 * y * dy) * 8 + (bit + dx - 2 * bit * dx) * 4 + lax.rem(z + dz, 4)
+        return slot, place * 8 + there
 
     def remote(src, dst, send_sem, recv_sem, target):
         pltpu.make_async_remote_copy(
@@ -171,13 +167,13 @@
     def scatter(e, by_i, matrix):
         blocks[e] = matrix.reshape(HEADS, HEAD_DIM, TOK)
         me = slot_i if by_i else slot_j
-        for offset in GROUP_OFFSETS:
+        for offset in sorted(GROUP_OFFSETS, key=lambda o: o[1]):
             slot, place = member(by_i, offset)
             remote(
                 blocks.at[e, rows_by[offset[1:]]],
                 arrived.at[e, me],
                 send.at[e],
-                recv.at[e, offset[0]],
+                recv.at[e, offset[1]],
                 {"lon": place},
             )
         arrived[e, me] = blocks[e, row]
@@ -190,7 +186,7 @@
         slot, place = member(by_i, offset)
         parts[p, slot] = block
         remote(
-            parts.at[p, slot], arrived.at[e, me], send.at[e], recv.at[e, offset[0]], {"lon": place}
+            parts.at[p, slot], arrived.at[e, me], send.at[e], recv.at[e, offset[1]], {"lon": place}
         )
 
     def wait_near(e):
@@ -205,16 +201,17 @@
     def joined(e):
         wait_near(e)
         wait_far(e)
-        total = arrived[e, 0:HEADS].astype(F32) + arrived[e, HEADS:GROUP].astype(F32)
-        return total.reshape(D, TOK)
+        quarter = [arrived[e, 4 * q : 4 * q + 4].astype(F32) for q in range(4)]
+        total = jnp.concatenate([quarter[0] + quarter[1], quarter[2] + quarter[3]], axis=0)
+        return total.reshape(D, TOK).astype(BF16)
 
     def span(index, size):
         return pl.ds(pl.multiple_of(index * size, size), size)
 
     def quarters(by_i, one):
         bit = bit_i if by_i else bit_j
-        for dx, dy in ((1, 1), (1, 0), (0, 1), (0, 0)):
-            quarter = (bit + dx - 2 * bit * dx) * 2 + (y + dy - 2 * y * dy)
+        for dx, dy in ((1, 1), (0, 1), (1, 0), (0, 0)):
+            quarter = (y + dy - 2 * y * dy) * 2 + (bit + dx - 2 * bit * dx)
             one(quarter, dx, dy)
 
     lane = lax.broadcasted_iota(jnp.int32, (1, 128), 1)
@@ -276,6 +273,20 @@
     for k in range(1, N_LAT):
         greet({"lat": lax.rem(lat + k, N_LAT)})
 
+    start_loads(
+        [
+            (prec_hbm, prec_ref),
+            (cells_hbm, cells_ref),
+            (weights_hbm, weights_ref),
+            (innov_hbm, innov_ref),
+            (slope_hbm, slope_ref),
+            (w_obs_hbm, w_obs_ref),
+            (w_down_hbm, w_down_ref),
+            (w_out_hbm, w_out_ref),
+            (w_up_hbm, w_up_ref),
+            (w_value_hbm, w_value_ref),
+        ]
+    )
     loads[id(key_ref)].wait()
     keys_t = key_ref[...].astype(F32).T.astype(BF16)
     loads[id(query_ref)].wait()
@@ -292,20 +303,20 @@
             slot_lane < count_ref[0, 0, d], weights_ref[0, 0, :, d, :], 0.0
         )
         er_stage[d] = (innov_ref[0, 0, :, d, :] * prec_t).astype(BF16)
-
     pl.semaphore_wait(barrier, GROUP - 1 + HEADS + N_LAT - 1)
-
-    scatter(KEYS, False, keys_t)
     for k in range(1, N_LAT):
         p = lax.rem(lat + k, N_LAT)
         push(st_stage.at[p], st_arrived.at[lat], STENCILS, {"lat": p})
         push(er_stage.at[p], er_arrived.at[lat], ERRORS, {"lat": p})
     st_arrived[lat] = st_stage[lat]
     er_arrived[lat] = er_stage[lat]
+    scatter(KEYS, False, keys_t)
     scatter(QUERIES, True, queries_t)
 
     loads[id(slope_ref)].wait()
     slope_t[...] = slope_ref[...].astype(F32).T.astype(BF16)
+    for ref in (w_obs_ref, w_down_ref, w_out_ref, w_up_ref, w_value_ref):
+        loads[id(ref)].wait()
 
     drain(st_arrived.at[pl.ds(0, N_LAT - 1)], other_recv.at[STENCILS])
     token = lax.broadcasted_iota(jnp.int32, (TOK, SLOTS), 0).astype(F32)
@@ -319,50 +330,52 @@
             )
         columns.append(total)
     operator = jnp.concatenate(columns, axis=1)
-    gram = contract(operator, operator, 1, 1, HIGHEST)
     drain(er_arrived.at[pl.ds(0, N_LAT - 1)], other_recv.at[ERRORS])
     errors = jnp.concatenate([er_arrived[a] for a in range(N_LAT)], axis=1).astype(F32)
-    for ref in (w_obs_ref, w_down_ref, w_up_ref, w_out_ref, w_value_ref):
-        loads[id(ref)].wait()
-
-    def adjoint_out(grad_t, e):
-        g = mm(w_obs_ref[...], grad_t.astype(BF16))
-        back = (mm(w_down_ref[...], g.astype(BF16)) * slope_t[...].astype(F32)).astype(BF16)
-        middle = g + mm(w_up_ref[...], back)
-        scatter(e, True, mm(w_out_ref[...], middle.astype(BF16)).astype(BF16))
-        return middle
+
+    def adjoint_out(grad, e):
+        back = (mm(w_do[...], grad) * slope_t[...].astype(F32)).astype(BF16)
+        scatter(e, True, (mm(w_ou[...], back) + mm(w_oo[...], grad)).astype(BF16))
+        return back
+
+    def adjoint_middle(grad, back):
+        middle = mm(w_obs_ref[...], grad) + mm(w_up_ref[...], back)
+        return middle, values_of(middle)
+
+    def values_of(middle):
+        high = middle.astype(BF16)
+        low = (middle - high.astype(F32)).astype(BF16)
+        return mm(w_value_t[...], high) + mm(w_value_t[...], low)
 
     def adjoint_mix(e, back, p):
         wait_near(e)
-        upward = (half(e, bit_i).astype(F32) * scale_ref[:, span(bit_i, HALF // 2)]).astype(BF16)
-        half_sum[...] = mm(upward, mix[span(bit_i, HALF // 2), :])
+        upward = (half(e, near).astype(F32) * scale_ref[:, span(near, HALF // 2)]).astype(BF16)
+        half_sum[...] = mm(upward, mix[span(near, HALF // 2), :])
         wait_far(e)
-        rest = (half(e, bit_j).astype(F32) * scale_ref[:, span(bit_j, HALF // 2)]).astype(BF16)
+        if p == 0:
+            set_scale(far, STATS + 1)
+        rest = (half(e, far).astype(F32) * scale_ref[:, span(far, HALF // 2)]).astype(BF16)
 
         def one(quarter, dx, dy):
             cols = span(quarter, HALF // 4)
-            half_sum[:, cols] += mm(rest, mix[span(bit_j, HALF // 2), cols])
+            half_sum[:, cols] += mm(rest, mix[span(far, HALF // 2), cols])
             for dz in (2, 1, 3, 0):
                 piece = half_sum[:, span(quarter * 4 + lax.rem(z + dz, 4), TOK)]
                 send_part(back, p, False, (dx, dy, dz), piece.astype(BF16))
 
         quarters(False, one)
 
-    def adjoint_in(middle, e):
-        return (middle + mm(w_value_ref[...], joined(e).astype(BF16))).T
-
-    def tangent_out(v, e):
-        scatter(e, False, mm(v.astype(BF16), w_value_ref[...]).T.astype(BF16))
-
-    def tangent_mix(e, back, p):
+    def tangent_mix(e, back, p, between=None):
         wait_near(e)
-        half_sum[...] = contract(half(e, bit_j), mix[:, span(bit_j, HALF // 2)], 1, 1)
+        half_sum[...] = contract(half(e, near), mix[:, span(near, HALF // 2)], 1, 1)
+        if between is not None:
+            between(1)
         wait_far(e)
-        rest = half(e, bit_i)
+        rest = half(e, far)
 
         def one(quarter, dx, dy):
             cols = span(quarter, HALF // 4)
-            out = half_sum[:, cols] + contract(rest, mix[cols, span(bit_i, HALF // 2)], 1, 1)
+            out = half_sum[:, cols] + contract(rest, mix[cols, span(far, HALF // 2)], 1, 1)
             half_sum[:, cols] = out * scale_ref[:, cols]
             for dz in (2, 1, 3, 0):
                 piece = half_sum[:, span(quarter * 4 + lax.rem(z + dz, 4), TOK)]
@@ -370,15 +383,24 @@
 
         quarters(True, one)
 
-    def tangent_in(v, attended):
-        after = v + mm(attended, w_out_ref[...])
-        hidden = (mm(after.astype(BF16), w_up_ref[...]) * slope_ref[...].astype(F32)).astype(BF16)
-        y_field = after + mm(hidden, w_down_ref[...])
-        field = mm(y_field.astype(BF16), w_obs_ref[...])
+    def tangent_start(v):
+        v_in = v.astype(BF16)
+        return mm(v_in, w_up_ref[...]), mm(v_in, w_obs_ref[...])
+
+    def tangent_in(started, attended):
+        hidden_v, field_v = started
+        hidden = hidden_v + mm(attended, w_ou[...])
+        hidden = (hidden * slope_ref[...].astype(F32)).astype(BF16)
+        field = field_v + mm(attended, w_oo[...]) + mm(hidden, w_do[...])
         grad_t = contract(field, gram, 0, 0, HIGHEST) * prec_t
         return field, grad_t
 
-    middle = adjoint_out(contract(errors, operator, 1, 1, HIGHEST), UP0)
+    grad = contract(errors, operator, 1, 1, HIGHEST).astype(BF16)
+    start = mm(w_obs_ref[...], grad)
+    back = (mm(w_down_ref[...], start.astype(BF16)) * slope_t[...].astype(F32)).astype(BF16)
+    middle = start + mm(w_up_ref[...], back)
+    scatter(UP0, True, mm(w_out_ref[...], middle.astype(BF16)).astype(BF16))
+    gram = contract(operator, operator, 1, 1, HIGHEST)
 
     wait_near(KEYS)
     wait_far(KEYS)
@@ -417,51 +439,68 @@
         )
 
     wait_near(QUERIES)
+    score_half(near, STATS)
     wait_far(QUERIES)
-    score_half(0, STATS)
-    score_half(1, STATS + 1)
-    set_scale(0, STATS)
-    set_scale(1, STATS + 1)
+    score_half(far, STATS + 1)
+    set_scale(near, STATS)
 
     adjoint_mix(UP0, BACK0, 0)
-    r1 = adjoint_in(middle, BACK0)
-
-    tangent_out(r1, VAL1)
+
+    w_value_t[...] = w_value_ref[...].astype(F32).T.astype(BF16)
+    w_vv[...] = mm(w_value_t[...], w_value_ref[...]).astype(BF16)
+    middle_values = values_of(middle)
+    w_do[...] = mm(w_down_ref[...], w_obs_ref[...]).astype(BF16)
+    w_oo[...] = mm(w_out_ref[...], w_obs_ref[...]).astype(BF16)
+    w_ou[...] = mm(w_out_ref[...], w_up_ref[...]).astype(BF16)
+    spread = joined(BACK0)
+
+    values1 = middle_values + mm(w_vv[...], spread)
+    scatter(VAL1, False, values1.astype(BF16))
+    r1 = (middle + mm(w_value_ref[...], spread)).T
     rr1 = total_of(r1 * r1)
     tangent_mix(VAL1, ATT1, 1)
-    attended1 = joined(ATT1).T
-    field, grad_t = tangent_in(r1, attended1.astype(BF16))
+    started = tangent_start(r1)
+    attended1 = joined(ATT1).astype(F32).T
+    field, grad_t = tangent_in(started, attended1.astype(BF16))
+    grad = grad_t.astype(BF16)
     sum_start(0, [rr1, total_of(field * grad_t.T)])
-    middle = adjoint_out(grad_t, UP1)
+    back = adjoint_out(grad, UP1)
     sum_middle(0)
+    middle, middle_values = adjoint_middle(grad, back)
     adjoint_mix(UP1, BACK1, 2)
     sum_last(0)
-    applied = r1 + adjoint_in(middle, BACK1)
     norm1, seen1 = sum_end(0, 2)
     step1 = norm1 / (norm1 + seen1)
+    values2 = values1 - step1 * (values1 + middle_values)
+    spread = joined(BACK1)
+
+    values2 = values2 - step1 * mm(w_vv[...], spread)
+    scatter(VAL2, False, values2.astype(BF16))
+    applied = r1 + (middle + mm(w_value_ref[...], spread)).T
     r2 = r1 - step1 * applied
-
-    tangent_out(r2, VAL2)
     sum_start(1, [total_of(r2 * r2)])
-    sum_middle(1)
-    tangent_mix(VAL2, ATT2, 3)
+    tangent_mix(VAL2, ATT2, 3, sum_middle)
     sum_last(1)
-    attended2 = joined(ATT2).T
     (norm2,) = sum_end(1, 1)
     beta = norm2 / norm1
     d2 = r2 + beta * r1
-    attended2 = attended2 + beta * attended1
-    field, grad_t = tangent_in(d2, attended2.astype(BF16))
+    started = tangent_start(d2)
+    attended2 = joined(ATT2).astype(F32).T + beta * attended1
+    field, grad_t = tangent_in(started, attended2.astype(BF16))
+    grad = grad_t.astype(BF16)
     sum_start(2, [total_of(d2 * d2), total_of(field * grad_t.T)])
-    middle = adjoint_out(grad_t, UP2)
+    back = adjoint_out(grad, UP2)
     sum_middle(2)
+    middle = mm(w_obs_ref[...], grad) + mm(w_up_ref[...], back)
+    base = (d2 + middle.T)
     adjoint_mix(UP2, BACK2, 4)
     sum_last(2)
-    applied = d2 + adjoint_in(middle, BACK2)
     squared2, seen2 = sum_end(2, 2)
     step2 = norm2 / (squared2 + seen2)
     sol_ref[...] = step1 * r1 + step2 * d2
-    res_ref[...] = r2 - step2 * applied
+    base = r2 - step2 * base
+    spread = joined(BACK2)
+    res_ref[...] = base - step2 * mm(w_value_ref[...], spread).T
 
     for e in range(N_EXCHANGES):
         drain(arrived.at[e, pl.ds(0, GROUP - 1)], send.at[e])
@@ -484,7 +523,7 @@
     in_specs[10] = pl.BlockSpec(memory_space=pltpu.SMEM)
     return pl.pallas_call(
         kernel,
-        out_shape=(jax.ShapeDtypeStruct((TOK, D), F32),) * 2,
+        out_shape=(pltpu.VMEM((TOK, D), F32),) * 2,
         in_specs=in_specs,
         out_specs=(vmem, vmem),
         scratch_shapes=[
@@ -498,6 +537,11 @@
             pltpu.VMEM((8, HALF), F32),
             pltpu.VMEM((1, HALF), F32),
             pltpu.VMEM((FF, TOK), BF16),
+            pltpu.VMEM((FF, CHANNELS), BF16),
+            pltpu.VMEM((D, CHANNELS), BF16),
+            pltpu.VMEM((D, FF), BF16),
+            pltpu.VMEM((D, D), BF16),
+            pltpu.VMEM((D, D), BF16),
             pltpu.VMEM((N_LAT, 2 * STENCIL, SLOTS), F32),
             pltpu.VMEM((N_LAT, 2 * STENCIL, SLOTS), F32),
             pltpu.VMEM((N_LAT, CHANNELS, SLOTS), BF16),

time: 97.6 us -> 89.7 us (0.919)
  Pallas kernels: 93.4 us -> 87.6 us
  local copies, waits for them, and re-layouts: 3.34 us -> 1.41 us
    pallas_call x1, Pallas kernels: 93.4 us -> 87.6 us  [per_device(): pl.pallas_call(kernel, out_shape=(pltpu.VMEM((TOK, D), F32),) * 2, in_spe...]
    unnamed x2, local copies, waits for them, and re-layouts: 3.34 us -> 1.41 us
where the time goes in v3:
time: 89.7 us; the launch traced here: 89.6 us
  Pallas kernels  87.6 us (98%)
  local copies, waits for them, and re-layouts  1.41 us (2%)
    pallas_call x1, Pallas kernels, per_device(): pl.pallas_call(kernel, out_shape=(pltpu.VMEM((TOK, D), F32),) * 2, in_spe...  87.6 us

profile of v3, /device:TPU:0, one launch (start us, length us, event | category | flops | bytes accessed | tf_op | source)
XLA Modules:
  0.0 89.6 jit_solution(7377462393109225474)
XLA Ops:
  0.6 87.6 %shard_map.140 = (f32[128,512]{1,0:T(8,128)S(1)}, f32[128,512]{1,0:T(8,128)S(1)}) custom-call(bf16[128,512]{1,0:T(8,128)(2,1)} %query_hbm.1, bf16[128,512]{1,0:T(8,128)(2,1)} %key_hbm.1, bf16[128,2048]{1,0:T(8,128)(2,1)} %slope_hbm.1, bf16[512,512]{1,0:T(8,128)(2,1)} %w_value_hbm.1, bf16[512,512]{1,0:T(8,128)(2,1)} %w_out_hbm.1, bf16[512,2048]{1,0:T(8,128)(2,1)} %w_up_hbm.1, ...), custom_call_target="tpu_custom_call" | custom-call | tf_op jit(solution)/shard_map/pallas_call | solution.py:524
  88.2 0.7 copy.17
  88.9 0.7 copy.18

commit v4 on v3

--- a/solution.py
+++ b/solution.py
@@ -28,7 +28,7 @@
 KEYS, QUERIES, UP0, BACK0, VAL1, ATT1, UP1, BACK1, VAL2, ATT2, UP2, BACK2 = range(12)
 N_EXCHANGES = 12
 STENCILS, ERRORS, STATS, SUMS = 0, 1, 2, 4
-N_SUMS = 3
+N_SUMS = 2
 N_OTHER = SUMS + 3 * N_SUMS
 
 
@@ -91,6 +91,7 @@
     parts,
     half_sum,
     mix,
+    mix_t,
     stat_mine,
     stat_other,
     scale_ref,
@@ -365,17 +366,15 @@
 
         quarters(False, one)
 
-    def tangent_mix(e, back, p, between=None):
+    def tangent_mix(e, back, p):
         wait_near(e)
-        half_sum[...] = contract(half(e, near), mix[:, span(near, HALF // 2)], 1, 1)
-        if between is not None:
-            between(1)
+        half_sum[...] = mm(half(e, near), mix_t[span(near, HALF // 2), :])
         wait_far(e)
         rest = half(e, far)
 
         def one(quarter, dx, dy):
             cols = span(quarter, HALF // 4)
-            out = half_sum[:, cols] + contract(rest, mix[cols, span(far, HALF // 2)], 1, 1)
+            out = half_sum[:, cols] + mm(rest, mix_t[span(far, HALF // 2), cols])
             half_sum[:, cols] = out * scale_ref[:, cols]
             for dz in (2, 1, 3, 0):
                 piece = half_sum[:, span(quarter * 4 + lax.rem(z + dz, 4), TOK)]
@@ -408,11 +407,17 @@
     keys = jnp.concatenate([arrived[KEYS, t] for t in range(GROUP)], axis=1)
     keys = jnp.concatenate([keys, keys], axis=0)
 
-    def score_rows(slot):
+    def query_of(slot):
         scaled = arrived[QUERIES, slot].astype(F32) * SCORE_SCALE
         high = scaled.astype(BF16)
         low = (scaled - high.astype(F32)).astype(BF16)
-        scores = contract(jnp.concatenate([high, low], axis=0), keys, 0, 0)
+        return jnp.concatenate([high, low], axis=0)
+
+    def keys_of(slot):
+        return jnp.concatenate([arrived[KEYS, slot], arrived[KEYS, slot]], axis=0)
+
+    def score_rows(slot):
+        scores = contract(query_of(slot), keys, 0, 0)
         top = jnp.max(scores, axis=1, keepdims=True)
         raised = jnp.exp2(scores - top)
         total = jnp.sum(raised, axis=1, keepdims=True)
@@ -457,13 +462,19 @@
     values1 = middle_values + mm(w_vv[...], spread)
     scatter(VAL1, False, values1.astype(BF16))
     r1 = (middle + mm(w_value_ref[...], spread)).T
+    queries = jnp.concatenate([query_of(t) for t in range(GROUP)], axis=1)
     rr1 = total_of(r1 * r1)
+    for t in range(GROUP):
+        mix_t[t * TOK : (t + 1) * TOK, :] = jnp.exp2(
+            contract(keys_of(t), queries, 0, 0) - stat_mine[0:1, :]
+        ).astype(BF16)
     tangent_mix(VAL1, ATT1, 1)
     started = tangent_start(r1)
-    attended1 = joined(ATT1).astype(F32).T
-    field, grad_t = tangent_in(started, attended1.astype(BF16))
+    attended = joined(ATT1).astype(F32).T.astype(BF16)
+    field, grad_t = tangent_in(started, attended)
     grad = grad_t.astype(BF16)
-    sum_start(0, [rr1, total_of(field * grad_t.T)])
+    grad_1 = grad_t.T
+    sum_start(0, [rr1, total_of(field * grad_1)])
     back = adjoint_out(grad, UP1)
     sum_middle(0)
     middle, middle_values = adjoint_middle(grad, back)
@@ -478,29 +489,27 @@
     scatter(VAL2, False, values2.astype(BF16))
     applied = r1 + (middle + mm(w_value_ref[...], spread)).T
     r2 = r1 - step1 * applied
-    sum_start(1, [total_of(r2 * r2)])
-    tangent_mix(VAL2, ATT2, 3, sum_middle)
+    tangent_mix(VAL2, ATT2, 3)
+    started = tangent_start(r2)
+    norms = [total_of(r2 * r2), total_of(r2 * r1)]
+    attended = joined(ATT2).astype(F32).T.astype(BF16)
+    field, grad_t = tangent_in(started, attended)
+    grad = grad_t.astype(BF16)
+    sum_start(1, norms + [total_of(field * grad_t.T), total_of(field * grad_1)])
+    back = adjoint_out(grad, UP2)
+    sum_middle(1)
+    partial = r2 + (mm(w_obs_ref[...], grad) + mm(w_up_ref[...], back)).T
+    adjoint_mix(UP2, BACK2, 4)
     sum_last(1)
-    (norm2,) = sum_end(1, 1)
+    norm2, cross2, seen2, cross_seen2 = sum_end(1, 4)
     beta = norm2 / norm1
-    d2 = r2 + beta * r1
-    started = tangent_start(d2)
-    attended2 = joined(ATT2).astype(F32).T + beta * attended1
-    field, grad_t = tangent_in(started, attended2.astype(BF16))
-    grad = grad_t.astype(BF16)
-    sum_start(2, [total_of(d2 * d2), total_of(field * grad_t.T)])
-    back = adjoint_out(grad, UP2)
-    sum_middle(2)
-    middle = mm(w_obs_ref[...], grad) + mm(w_up_ref[...], back)
-    base = (d2 + middle.T)
-    adjoint_mix(UP2, BACK2, 4)
-    sum_last(2)
-    squared2, seen2 = sum_end(2, 2)
-    step2 = norm2 / (squared2 + seen2)
-    sol_ref[...] = step1 * r1 + step2 * d2
-    base = r2 - step2 * base
+    step2 = norm2 / (
+        norm2 + seen2 + 2.0 * beta * (cross2 + cross_seen2) + beta * beta * (norm1 + seen1)
+    )
+    sol_ref[...] = step1 * r1 + step2 * (r2 + beta * r1)
+    partial = r2 - step2 * (partial + beta * applied)
     spread = joined(BACK2)
-    res_ref[...] = base - step2 * mm(w_value_ref[...], spread).T
+    res_ref[...] = partial - step2 * mm(w_value_ref[...], spread).T
 
     for e in range(N_EXCHANGES):
         drain(arrived.at[e, pl.ds(0, GROUP - 1)], send.at[e])
@@ -532,6 +541,7 @@
             pltpu.VMEM((N_EXCHANGES, HEADS, HEAD_DIM, TOK), BF16),
             pltpu.VMEM((5, GROUP, HEAD_DIM, TOK), BF16),
             pltpu.VMEM((HEAD_DIM, HALF), F32),
+            pltpu.VMEM((HALF, HALF), BF16),
             pltpu.VMEM((HALF, HALF), BF16),
             pltpu.VMEM((8, HALF), F32),
             pltpu.VMEM((8, HALF), F32),

time: 89.7 us -> 87.2 us (0.972)
  Pallas kernels: 87.6 us -> 85.1 us
    pallas_call x1, Pallas kernels: 87.6 us -> 85.1 us  [per_device(): pl.pallas_call(kernel, out_shape=(pltpu.VMEM((TOK, D), F32),) * 2, in_spe...]
where the time goes in v4:
time: 87.2 us; the launch traced here: 87.1 us
  Pallas kernels  85.1 us (98%)
  local copies, waits for them, and re-layouts  1.41 us (2%)
    pallas_call x1, Pallas kernels, per_device(): pl.pallas_call(kernel, out_shape=(pltpu.VMEM((TOK, D), F32),) * 2, in_spe...  85.1 us

profile of v4, /device:TPU:0, one launch (start us, length us, event | category | flops | bytes accessed | tf_op | source)
XLA Modules:
  0.0 87.1 jit_solution(17541353623486624417)
XLA Ops:
  0.6 85.1 %shard_map.140 = (f32[128,512]{1,0:T(8,128)S(1)}, f32[128,512]{1,0:T(8,128)S(1)}) custom-call(bf16[128,512]{1,0:T(8,128)(2,1)} %query_hbm.1, bf16[128,512]{1,0:T(8,128)(2,1)} %key_hbm.1, bf16[128,2048]{1,0:T(8,128)(2,1)} %slope_hbm.1, bf16[512,512]{1,0:T(8,128)(2,1)} %w_value_hbm.1, bf16[512,512]{1,0:T(8,128)(2,1)} %w_out_hbm.1, bf16[512,2048]{1,0:T(8,128)(2,1)} %w_up_hbm.1, ...), custom_call_target="tpu_custom_call" | custom-call | tf_op jit(solution)/shard_map/pallas_call | solution.py:533
  85.7 0.7 copy.17
  86.4 0.7 copy.18

commit v5 on v4

--- a/solution.py
+++ b/solution.py
@@ -461,14 +461,14 @@
 
     values1 = middle_values + mm(w_vv[...], spread)
     scatter(VAL1, False, values1.astype(BF16))
-    r1 = (middle + mm(w_value_ref[...], spread)).T
     queries = jnp.concatenate([query_of(t) for t in range(GROUP)], axis=1)
-    rr1 = total_of(r1 * r1)
     for t in range(GROUP):
         mix_t[t * TOK : (t + 1) * TOK, :] = jnp.exp2(
             contract(keys_of(t), queries, 0, 0) - stat_mine[0:1, :]
         ).astype(BF16)
     tangent_mix(VAL1, ATT1, 1)
+    r1 = (middle + mm(w_value_ref[...], spread)).T
+    rr1 = total_of(r1 * r1)
     started = tangent_start(r1)
     attended = joined(ATT1).astype(F32).T.astype(BF16)
     field, grad_t = tangent_in(started, attended)
@@ -487,9 +487,9 @@
 
     values2 = values2 - step1 * mm(w_vv[...], spread)
     scatter(VAL2, False, values2.astype(BF16))
+    tangent_mix(VAL2, ATT2, 3)
     applied = r1 + (middle + mm(w_value_ref[...], spread)).T
     r2 = r1 - step1 * applied
-    tangent_mix(VAL2, ATT2, 3)
     started = tangent_start(r2)
     norms = [total_of(r2 * r2), total_of(r2 * r1)]
     attended = joined(ATT2).astype(F32).T.astype(BF16)

time: 87.2 us -> 87.3 us (level)
  no operation moved by 1% of the time
where the time goes in v5:
time: 87.3 us; the launch traced here: 87.2 us
  Pallas kernels  85.1 us (97%)
  local copies, waits for them, and re-layouts  1.41 us (2%)
    pallas_call x1, Pallas kernels, per_device(): pl.pallas_call(kernel, out_shape=(pltpu.VMEM((TOK, D), F32),) * 2, in_spe...  85.1 us

profile of v5, /device:TPU:0, one launch (start us, length us, event | category | flops | bytes accessed | tf_op | source)
XLA Modules:
  0.0 87.2 jit_solution(5147057319270606096)
XLA Ops:
  0.6 85.1 %shard_map.140 = (f32[128,512]{1,0:T(8,128)S(1)}, f32[128,512]{1,0:T(8,128)S(1)}) custom-call(bf16[128,512]{1,0:T(8,128)(2,1)} %query_hbm.1, bf16[128,512]{1,0:T(8,128)(2,1)} %key_hbm.1, bf16[128,2048]{1,0:T(8,128)(2,1)} %slope_hbm.1, bf16[512,512]{1,0:T(8,128)(2,1)} %w_value_hbm.1, bf16[512,512]{1,0:T(8,128)(2,1)} %w_out_hbm.1, bf16[512,2048]{1,0:T(8,128)(2,1)} %w_up_hbm.1, ...), custom_call_target="tpu_custom_call" | custom-call | tf_op jit(solution)/shard_map/pallas_call | solution.py:533
  85.8 0.7 copy.17
  86.5 0.7 copy.18
